TPU v7x, 32 devices: a whole 2x2x4 slice. The times are simulated.
32 devices in a mesh: aux: 4 (over y, x), basis: 8 (over z, core).
Axes of the slice: x: 2, y: 2, z: 4, core: 2. Of those that a mesh axis runs over, the one named last changes fastest.
Arguments:
- factors: bfloat16 [16, 500, 8192], P('aux', None, 'basis'), may hold values from -0.125 to 0.125
Outputs:
- exchange_band: float32 [3, 8192, 1024], P(None, ('basis', 'aux'))
All inputs are finite; a program needn't handle non-finite values.
Results may differ from a plain program's by a relative error of at most 0.0003.
Values may be sent and summed in bfloat16 or wider, within the bound.
A program may use at most 64 MiB of HBM per device.

v0:
```python
import jax
import jax.numpy as jnp
from jax import lax
from jax.sharding import PartitionSpec as P

SHIFTS = 3


def from_behind(value, axis, steps):
    count = lax.axis_size(axis)
    pairs = [(source, (source + steps) % count) for source in range(count)]
    return lax.ppermute(value, axis, pairs)


def form_tile(own_flat, moving):
    other = moving.reshape(-1, moving.shape[2])
    return lax.dot_general(
        own_flat, other, (((0,), (0,)), ((), ())), preferred_element_type=jnp.float32
    )


def on_device(factors):
    own_flat = factors.reshape(-1, factors.shape[2])
    moving = factors
    results = []
    for s in range(SHIFTS):
        if s > 0:
            moving = from_behind(moving, "basis", -1)
        partial_tile = form_tile(own_flat, moving)
        results.append(partial_tile)
    stacked = jnp.stack(results)
    return lax.psum_scatter(stacked, "aux", scatter_dimension=1, tiled=True)


def solution(mesh):
    in_specs = (P("aux", None, "basis"),)
    out_specs = P(None, ("basis", "aux"), None)
    return jax.shard_map(
        on_device, mesh=mesh, in_specs=in_specs, out_specs=out_specs, check_vma=False
    )
```

profile of v0, /device:TPU:1, one launch (start us, length us, event | category | flops | bytes accessed | tf_op | source)
XLA Modules:
  0.0 247.2 jit_solution(18281692217060605504)
XLA Ops:
  6.5 0.0 reduce-scatter.2.cloned.1.call-start
  6.5 0.0 copy-start
  6.5 0.1 collective-permute-start
  6.6 48.0 %collective-permute-done = bf16[4,500,1024]{2,0,1:T(4,128)(2,1)S(1)} collective-permute-done((bf16[4,500,1024]{2,0,1:T(4,128)(2,1)}, bf16[4,500,1024]{2,0,1:T(4,128)(2,1)S(1)}, u32[]{:S(2)}, u32[]{:S(2)}) %collective-permute-start) | collective-permute-done | bytes 4096032 | tf_op jit(solution)/shard_map/ppermute | solution.py:12
  54.6 1.7 collective-permute-start.1
  56.4 11.1 %fusion.8 = f32[1,1024,1024]{2,1,0:T(8,128)S(1)} fusion(bf16[4,500,1024]{2,0,1:T(4,128)(2,1)} %param.1), kind=kOutput, calls=%fused_computation.9 | convolution fusion | flops 4194304000 | bytes 8290304 | tf_op jit(solution)/shard_map/dot_general | solution.py:17
  67.5 0.0 copy-done
  67.5 8.3 %fusion.11 = f32[1,1024,1024]{2,1,0:T(8,128)S(1)} fusion(bf16[4,500,1024]{2,0,1:T(4,128)(2,1)S(1)} %collective-permute-done, bf16[4,500,1024]{2,0,1:T(4,128)(2,1)S(1)} %copy-done), kind=kOutput, calls=%fused_computation.10 | convolution fusion | flops 4194304000 | bytes 12386304 | tf_op jit(solution)/shard_map/dot_general | solution.py:17
  75.9 25.6 %collective-permute-done.1 = bf16[4,500,1024]{2,0,1:T(4,128)(2,1)S(1)} collective-permute-done((bf16[4,500,1024]{2,0,1:T(4,128)(2,1)S(1)}, bf16[4,500,1024]{2,0,1:T(4,128)(2,1)S(1)}, u32[]{:S(2)}, u32[]{:S(2)}) %collective-permute-start.1) | collective-permute-done | bytes 4096032 | tf_op jit(solution)/shard_map/ppermute | solution.py:12
  101.5 8.5 %fusion.16 = f32[1,1024,1024]{2,1,0:T(8,128)S(1)} fusion(bf16[4,500,1024]{2,0,1:T(4,128)(2,1)S(1)} %collective-permute-done.1, bf16[4,500,1024]{2,0,1:T(4,128)(2,1)S(1)} %copy-done), kind=kOutput, calls=%fused_computation.11 | convolution fusion | flops 4194304000 | bytes 12386304 | tf_op jit(solution)/shard_map/dot_general | solution.py:17
  110.1 5.2 %pad_maximum_fusion = f32[3,1024,1024]{2,1,0:T(8,128)} fusion(f32[1,1024,1024]{2,1,0:T(8,128)S(1)} %fusion.16, f32[1,1024,1024]{2,1,0:T(8,128)S(1)} %fusion.11, f32[1,1024,1024]{2,1,0:T(8,128)S(1)} %fusion.8), kind=kLoop, calls=%fused_computation | loop fusion | flops 6291456 | bytes 25165824 | tf_op jit(solution)/shard_map/stack | solution.py:31
  115.3 0.0 reduce-scatter.2.cloned.1.call-update
  115.3 125.0 %reduce-scatter.2.cloned.1.call-done = f32[3,256,1024]{2,1,0:T(8,128)} async-done(((f32[3,1024,1024]{2,1,0:T(8,128)}), f32[3,256,1024]{2,1,0:T(8,128)}) %reduce-scatter.2.cloned.1.call-update) | async-done | bytes 3145744 | tf_op jit(solution)/shard_map/reduce_scatter | solution.py:32
Async XLA Ops:
  6.5 233.8 %reduce-scatter.2.cloned.1.call-start = ((), (), s32[]{:S(2)}) async-start(), calls=%async_computation.1 | async-start | bytes 15728640 | tf_op jit(solution)/shard_map/reduce_scatter | solution.py:32
  6.5 61.0 %copy-start = (bf16[4,500,1024]{2,0,1:T(4,128)(2,1)S(1)}, bf16[4,500,1024]{2,0,1:T(4,128)(2,1)}, u32[]{:S(2)}) copy-start(bf16[4,500,1024]{2,0,1:T(4,128)(2,1)} %param.1) | copy-start | bytes 12288004
  6.5 48.1 %collective-permute-start = (bf16[4,500,1024]{2,0,1:T(4,128)(2,1)}, bf16[4,500,1024]{2,0,1:T(4,128)(2,1)S(1)}, u32[]{:S(2)}, u32[]{:S(2)}) collective-permute-start(bf16[4,500,1024]{2,0,1:T(4,128)(2,1)} %param.1), channel_id=1, source_target_pairs={{0,7},{1,0},{2,1},{3,2},{4,3},{5,4},{6,5},{7,6},{8,15},{9,8},{10,9... | collective-permute-start | bytes 12288008 | tf_op jit(solution)/shard_map/ppermute | solution.py:12
  54.6 46.9 %collective-permute-start.1 = (bf16[4,500,1024]{2,0,1:T(4,128)(2,1)S(1)}, bf16[4,500,1024]{2,0,1:T(4,128)(2,1)S(1)}, u32[]{:S(2)}, u32[]{:S(2)}) collective-permute-start(bf16[4,500,1024]{2,0,1:T(4,128)(2,1)S(1)} %collective-permute-done), channel_id=1, source_target_pairs={{0,7},{1,0},{2,1},{3,2},{4,3},{5,4},{6,5},{7,6},{8,15},{9,8},{10,9... | collective-permute-start | bytes 12288008 | tf_op jit(solution)/shard_map/ppermute | solution.py:12
Sparse Core Ops, SparseCore 0:
  115.4 124.8 reduce-scatter.1
where the time goes:
time: 248 us; the launch traced here: 247 us
  waiting for transfers between devices  199 us (80%)
  matrix products  28 us (11%)
  between operations  13.4 us (5%)
  other arithmetic  5.22 us (2%)
    reduce_scatter x1, waiting for transfers between devices, on_device(): return lax.psum_scatter(stacked, 'aux', scatter_dimension=1, tiled=True)  125 us
    ppermute x2, waiting for transfers between devices, from_behind(): return lax.ppermute(value, axis, pairs)  73.7 us
    dot_general x3, matrix products, form_tile(): lax.dot_general(own_flat, other, (((0,), (0,)), ((), ())), preferred_elem...  28 us
    another operation x1, other arithmetic, on_device(): stacked = jnp.stack(results)  5.22 us
  transfers between devices with their start and end apart: 3, of which 3 were waited for; matrix products, arithmetic and copies ran while one was open for 8% of the time, Pallas kernels for 0%

commit v1 on v0

v1 whole, which is shorter than its diff:
```python
import functools

import jax
import jax.numpy as jnp
from jax import lax
from jax.experimental import pallas as pl
from jax.experimental.pallas import tpu as pltpu
from jax.sharding import PartitionSpec as P

SHIFTS = 3
MESH = pl.DeviceIdType.MESH


def round_up(value, step):
    return -(-value // step) * step


def kernel(cfg, x_ref, out_ref, own_t, got, part, *rest):
    depth, full, block, width, chunks, bits, n_aux, n_basis = cfg
    hop_refs = rest[: 2 * bits]
    ring_send, ring_recv, hop_send, hop_recv = rest[2 * bits :]
    half = width // 2
    rows = block // n_aux
    me_aux = lax.axis_index("aux")
    me_basis = lax.axis_index("basis")
    left = lax.rem(me_basis + n_basis - 1, n_basis)
    right = lax.rem(me_basis + 1, n_basis)
    my_bit = [lax.rem(me_aux // (2**q), 2) for q in range(bits)]
    partner = [me_aux + (1 - 2 * my_bit[q]) * 2**q for q in range(bits)]

    barrier = pltpu.get_barrier_semaphore()
    for who in [{"basis": left}, {"basis": right}] + [{"aux": p} for p in partner]:
        pl.semaphore_signal(barrier, inc=1, device_id=who, device_id_type=MESH)
    if full > depth:
        for s in range(SHIFTS - 1):
            got[s, depth:full, :] = jnp.zeros((full - depth, block), got.dtype)
    pl.semaphore_wait(barrier, 2 + bits)

    def ring_copy(s, j):
        cols = pl.ds(j * width, width)
        source = x_ref if s == 0 else got.at[s - 1]
        return pltpu.make_async_remote_copy(
            src_ref=source.at[pl.ds(0, depth), cols],
            dst_ref=got.at[s, pl.ds(0, depth), cols],
            send_sem=ring_send.at[s, j],
            recv_sem=ring_recv.at[s, j],
            device_id={"basis": left},
            device_id_type=MESH,
        )

    def order(side):
        return list(range(bits)) if side == 0 else list(range(bits))[::-1]

    def cut(side, hop, last):
        index = [pl.ds(0, 2)] * bits
        for step, q in enumerate(order(side)[: hop + 1]):
            index[bits - 1 - q] = my_bit[q] if step < hop or not last else 1 - my_bit[q]
        return tuple(index)

    def hop_copy(n, side, hop):
        q = order(side)[hop]
        return pltpu.make_async_remote_copy(
            src_ref=part.at[(n, side) + cut(side, hop, True)],
            dst_ref=hop_refs[side * bits + hop].at[n],
            send_sem=hop_send.at[n, side, hop],
            recv_sem=hop_recv.at[n, side, hop],
            device_id={"aux": partner[q]},
            device_id_type=MESH,
        )

    for j in range(chunks):
        ring_copy(0, j).start()

    step_cols = 128
    for i in range(block // step_cols):
        cols = pl.ds(i * step_cols, step_cols)
        own_t[cols, :] = x_ref[:, cols].T

    tiles = [(s, j) for s in range(SHIFTS) for j in range(chunks)]
    lhs_rows = min(256, block)

    def compute(n):
        s, j = tiles[n]
        cols = pl.ds(j * width, width)

        def body(i, carry):
            here = pl.ds(pl.multiple_of(i * lhs_rows, lhs_rows), lhs_rows)
            other = x_ref[:, cols] if s == 0 else got[s - 1, :, cols]
            product = jnp.dot(
                own_t[here, :], other, preferred_element_type=jnp.float32
            )
            per = lhs_rows // rows
            for r in range(per):
                g = i * per + r
                index = [lax.rem(g // (2**q), 2) for q in range(bits)][::-1]
                for side in range(2):
                    part[(n, side) + tuple(index)] = product[
                        r * rows : (r + 1) * rows, side * half : (side + 1) * half
                    ]
            return carry

        lax.fori_loop(0, block // lhs_rows, body, 0)

    def finish(n, hop):
        s, j = tiles[n]
        for side in range(2):
            hop_copy(n, side, hop).wait_recv()
            index = (n, side) + cut(side, hop, False)
            total = part[index] + hop_refs[side * bits + hop][n]
            if hop < bits - 1:
                part[index] = total
                hop_copy(n, side, hop + 1).start()
            else:
                out_ref[s, :, j * width + side * half : j * width + (side + 1) * half] = total

    count = len(tiles)
    lag = 2
    for n in range(count + lag * bits):
        if n < count:
            s, j = tiles[n]
            if s > 0:
                ring_copy(s - 1, j).wait_recv()
                if s < SHIFTS - 1:
                    ring_copy(s, j).start()
            compute(n)
            for side in range(2):
                hop_copy(n, side, 0).start()
        for hop in range(bits):
            m = n - lag * (hop + 1)
            if 0 <= m < count:
                finish(m, hop)

    for s in range(SHIFTS - 1):
        for j in range(chunks):
            ring_copy(s, j).wait_send()
    for n in range(count):
        for side in range(2):
            for hop in range(bits):
                hop_copy(n, side, hop).wait_send()


def on_device(n_aux, n_basis, factors):
    depth = factors.shape[0] * factors.shape[1]
    block = factors.shape[2]
    full = round_up(depth, 256)
    flat = jnp.pad(factors.reshape(depth, block), ((0, full - depth), (0, 0)))
    bits = n_aux.bit_length() - 1
    width = 256
    chunks = block // width
    count = SHIFTS * chunks
    rows = block // n_aux
    half = width // 2
    hop_bufs = []
    for side in range(2):
        for hop in range(bits):
            shape = (count,) + (2,) * (bits - 1 - hop) + (rows, half)
            hop_bufs.append(pltpu.VMEM(shape, jnp.float32))
    cfg = (depth, full, block, width, chunks, bits, n_aux, n_basis)
    return pl.pallas_call(
        functools.partial(kernel, cfg),
        out_shape=jax.ShapeDtypeStruct((SHIFTS, rows, block), jnp.float32),
        in_specs=[pl.BlockSpec(memory_space=pltpu.VMEM)],
        out_specs=pl.BlockSpec(memory_space=pltpu.VMEM),
        scratch_shapes=[
            pltpu.VMEM((block, full), jnp.bfloat16),
            pltpu.VMEM((SHIFTS - 1, full, block), jnp.bfloat16),
            pltpu.VMEM((count, 2) + (2,) * bits + (rows, half), jnp.float32),
            *hop_bufs,
            pltpu.SemaphoreType.DMA((SHIFTS - 1, chunks)),
            pltpu.SemaphoreType.DMA((SHIFTS - 1, chunks)),
            pltpu.SemaphoreType.DMA((count, 2, bits)),
            pltpu.SemaphoreType.DMA((count, 2, bits)),
        ],
        compiler_params=pltpu.CompilerParams(
            collective_id=0, has_side_effects=True, vmem_limit_bytes=58 * 2**20
        ),
        cost_estimate=pl.CostEstimate(
            flops=2 * SHIFTS * full * block * block,
            bytes_accessed=2 * full * block + 4 * SHIFTS * rows * block,
            transcendentals=0,
        ),
    )(flat)


def solution(mesh):
    n_aux, n_basis = mesh.shape["aux"], mesh.shape["basis"]
    return jax.shard_map(
        functools.partial(on_device, n_aux, n_basis),
        mesh=mesh,
        in_specs=(P("aux", None, "basis"),),
        out_specs=P(None, ("basis", "aux"), None),
        check_vma=False,
    )
```

time: 248 us -> 132 us (0.53)
  waiting for transfers between devices: 199 us -> 0 us
  Pallas kernels: 0 us -> 114 us
  matrix products: 28 us -> 0 us
  local copies, waits for them, and re-layouts: 0.01 us -> 17.8 us
  between operations: 13.4 us -> 0.01 us
  other arithmetic: 5.22 us -> 0 us
    reduce_scatter x1 -> x0, waiting for transfers between devices: 125 us -> none  [on_device(): return lax.psum_scatter(stacked, 'aux', scatter_dimension=1, tiled=True)]
    pallas_call x0 -> x1, Pallas kernels: none -> 114 us  [on_device(): pl.pallas_call(functools.partial(kernel, cfg), out_shape=jax.ShapeDtypeSt...]
    ppermute x2 -> x0, waiting for transfers between devices: 73.7 us -> none  [from_behind(): return lax.ppermute(value, axis, pairs)]
    dot_general x3 -> x0, matrix products: 28 us -> none  [form_tile(): lax.dot_general(own_flat, other, (((0,), (0,)), ((), ())), preferred_elem...]
    unnamed x2, local copies, waits for them, and re-layouts: 0.01 us -> 9.38 us
    another operation x1 -> x0, other arithmetic: 5.22 us -> none  [on_device(): stacked = jnp.stack(results)]
    pad x0 -> x1, local copies, waits for them, and re-layouts: none -> 4.52 us  [on_device(): flat = jnp.pad(factors.reshape(depth, block), ((0, full - depth), (0, 0)))]
    reshape x0 -> x1, local copies, waits for them, and re-layouts: none -> 3.92 us  [on_device(): flat = jnp.pad(factors.reshape(depth, block), ((0, full - depth), (0, 0)))]
  transfers between devices with their start and end apart: 3 -> 0, of which waited for: 3 -> 0; matrix products, arithmetic and copies ran while one was open for 8% -> 0% of each run, Pallas kernels for 0% -> 0%
where the time goes in v1:
time: 132 us
  Pallas kernels  114 us (86%)
  local copies, waits for them, and re-layouts  17.8 us (13%)
    pallas_call x1, Pallas kernels, on_device(): pl.pallas_call(functools.partial(kernel, cfg), out_shape=jax.ShapeDtypeSt...  114 us
    unnamed x2, local copies, waits for them, and re-layouts  9.38 us
    pad x1, local copies, waits for them, and re-layouts, on_device(): flat = jnp.pad(factors.reshape(depth, block), ((0, full - depth), (0, 0)))  4.52 us
    reshape x1, local copies, waits for them, and re-layouts, on_device(): flat = jnp.pad(factors.reshape(depth, block), ((0, full - depth), (0, 0)))  3.92 us

profile of v1, /device:TPU:1, one launch (start us, length us, event | category | flops | bytes accessed | tf_op | source)
XLA Modules:
  0.0 131.8 jit_solution(17913768761658748472)
XLA Ops:
  0.0 5.4 %copy.3 = bf16[4,500,1024]{2,1,0:T(8,128)(2,1)} copy(bf16[4,500,1024]{2,0,1:T(4,128)(2,1)} %param.1) | data formatting | bytes 8192000 | tf_op args[0]
  5.4 3.9 %reshape.3 = bf16[2000,1024]{1,0:T(8,128)(2,1)} reshape(bf16[4,500,1024]{2,1,0:T(8,128)(2,1)} %copy.3) | data formatting | bytes 8192000 | tf_op jit(solution)/shard_map/reshape | solution.py:146
  9.3 4.5 %pad.4.x_ref = bf16[2048,1024]{1,0:T(8,128)(2,1)} pad(bf16[2000,1024]{1,0:T(8,128)(2,1)} %reshape.3, bf16[]{:T(256)} %constant.2.clone.1), padding=0_48x0_0 | pad | bytes 8290306 | tf_op jit(solution)/shard_map/jit(_pad)/pad | solution.py:146
  13.9 114.0 %shard_map.17 = f32[3,256,1024]{2,1,0:T(8,128)} custom-call(bf16[2048,1024]{1,0:T(8,128)(2,1)} %pad.4.x_ref), custom_call_target="tpu_custom_call" | custom-call | flops 12884901888 | bytes 7340032 | tf_op jit(solution)/shard_map/pallas_call | solution.py:159
  127.8 4.0 %copy.5 = f32[3,256,1024]{2,1,0:T(8,128)} copy(f32[3,256,1024]{2,1,0:T(8,128)} %shard_map.17) | data formatting | bytes 6291456

commit v2 on v1

--- a/solution.py
+++ b/solution.py
@@ -15,10 +15,10 @@
     return -(-value // step) * step
 
 
-def kernel(cfg, x_ref, out_ref, own_t, got, part, *rest):
+def kernel(cfg, x_hbm, out_ref, x_ref, own_t, got, part, *rest):
     depth, full, block, width, chunks, bits, n_aux, n_basis = cfg
     hop_refs = rest[: 2 * bits]
-    ring_send, ring_recv, hop_send, hop_recv = rest[2 * bits :]
+    load_sem, ring_send, ring_recv, hop_send, hop_recv = rest[2 * bits :]
     half = width // 2
     rows = block // n_aux
     me_aux = lax.axis_index("aux")
@@ -28,12 +28,20 @@
     my_bit = [lax.rem(me_aux // (2**q), 2) for q in range(bits)]
     partner = [me_aux + (1 - 2 * my_bit[q]) * 2**q for q in range(bits)]
 
+    def load(j):
+        here = (pl.ds(0, depth), pl.ds(j * width, width))
+        return pltpu.make_async_copy(x_hbm.at[here], x_ref.at[here], load_sem.at[j])
+
+    for j in range(chunks):
+        load(j).start()
+
     barrier = pltpu.get_barrier_semaphore()
     for who in [{"basis": left}, {"basis": right}] + [{"aux": p} for p in partner]:
         pl.semaphore_signal(barrier, inc=1, device_id=who, device_id_type=MESH)
     if full > depth:
         for s in range(SHIFTS - 1):
             got[s, depth:full, :] = jnp.zeros((full - depth, block), got.dtype)
+        x_ref[depth:full, :] = jnp.zeros((full - depth, block), x_ref.dtype)
     pl.semaphore_wait(barrier, 2 + bits)
 
     def ring_copy(s, j):
@@ -69,6 +77,7 @@
         )
 
     for j in range(chunks):
+        load(j).wait()
         ring_copy(0, j).start()
 
     step_cols = 128
@@ -143,7 +152,7 @@
     depth = factors.shape[0] * factors.shape[1]
     block = factors.shape[2]
     full = round_up(depth, 256)
-    flat = jnp.pad(factors.reshape(depth, block), ((0, full - depth), (0, 0)))
+    flat = jnp.transpose(factors, (1, 0, 2)).reshape(depth, block)
     bits = n_aux.bit_length() - 1
     width = 256
     chunks = block // width
@@ -159,13 +168,15 @@
     return pl.pallas_call(
         functools.partial(kernel, cfg),
         out_shape=jax.ShapeDtypeStruct((SHIFTS, rows, block), jnp.float32),
-        in_specs=[pl.BlockSpec(memory_space=pltpu.VMEM)],
+        in_specs=[pl.BlockSpec(memory_space=pl.ANY)],
         out_specs=pl.BlockSpec(memory_space=pltpu.VMEM),
         scratch_shapes=[
+            pltpu.VMEM((full, block), jnp.bfloat16),
             pltpu.VMEM((block, full), jnp.bfloat16),
             pltpu.VMEM((SHIFTS - 1, full, block), jnp.bfloat16),
             pltpu.VMEM((count, 2) + (2,) * bits + (rows, half), jnp.float32),
             *hop_bufs,
+            pltpu.SemaphoreType.DMA((chunks,)),
             pltpu.SemaphoreType.DMA((SHIFTS - 1, chunks)),
             pltpu.SemaphoreType.DMA((SHIFTS - 1, chunks)),
             pltpu.SemaphoreType.DMA((count, 2, bits)),

time: 132 us -> 124 us (0.939)
  local copies, waits for them, and re-layouts: 17.8 us -> 11.4 us
  Pallas kernels: 114 us -> 112 us
    unnamed x2 -> x1, local copies, waits for them, and re-layouts: 9.38 us -> 3.97 us
    pad x1 -> x0, local copies, waits for them, and re-layouts: 4.52 us -> none  [on_device(): flat = jnp.pad(factors.reshape(depth, block), ((0, full - depth), (0, 0)))]
    reshape x1, local copies, waits for them, and re-layouts: 3.92 us -> 7.4 us  [on_device(): flat = jnp.transpose(factors, (1, 0, 2)).reshape(depth, block)]
    pallas_call x1, Pallas kernels: 114 us -> 112 us  [on_device(): pl.pallas_call(functools.partial(kernel, cfg), out_shape=jax.ShapeDtypeSt...]
where the time goes in v2:
time: 124 us
  Pallas kernels  112 us (90%)
  local copies, waits for them, and re-layouts  11.4 us (9%)
    pallas_call x1, Pallas kernels, on_device(): pl.pallas_call(functools.partial(kernel, cfg), out_shape=jax.ShapeDtypeSt...  112 us
    reshape x1, local copies, waits for them, and re-layouts, on_device(): flat = jnp.transpose(factors, (1, 0, 2)).reshape(depth, block)  7.4 us
    unnamed x1, local copies, waits for them, and re-layouts  3.97 us

profile of v2, /device:TPU:1, one launch (start us, length us, event | category | flops | bytes accessed | tf_op | source)
XLA Modules:
  0.0 123.5 jit_solution(16068987265202477807)
XLA Ops:
  0.0 7.4 %reshape.3.x_hbm = bf16[2000,1024]{1,0:T(8,128)(2,1)} reshape(bf16[500,4,1024]{2,1,0:T(4,128)(2,1)} %bitcast.1) | data formatting | bytes 8192000 | tf_op jit(solution)/shard_map/reshape | solution.py:155
  7.4 112.1 %shard_map.17 = f32[3,256,1024]{2,1,0:T(8,128)} custom-call(bf16[2000,1024]{1,0:T(8,128)(2,1)} %reshape.3.x_hbm), custom_call_target="tpu_custom_call" | custom-call | flops 12884901888 | bytes 7340032 | tf_op jit(solution)/shard_map/pallas_call | solution.py:168
  119.6 4.0 %copy.3 = f32[3,256,1024]{2,1,0:T(8,128)} copy(f32[3,256,1024]{2,1,0:T(8,128)} %shard_map.17) | data formatting | bytes 6291456

commit v3 on v2

--- a/solution.py
+++ b/solution.py
@@ -8,6 +8,8 @@
 from jax.sharding import PartitionSpec as P
 
 SHIFTS = 3
+SMALLEST = 2.0**-125
+UNIT_ROWS = 16
 MESH = pl.DeviceIdType.MESH
 
 
@@ -15,10 +17,27 @@
     return -(-value // step) * step
 
 
-def kernel(cfg, x_hbm, out_ref, x_ref, own_t, got, part, *rest):
+def encode(value, unit):
+    scaled = value * (1.0 / unit)
+    power = scaled * scaled
+    power = power * power
+    power = power * power
+    return jnp.where(scaled < 0, -power, power).astype(jnp.bfloat16)
+
+
+def decode(code, unit):
+    code = code.astype(jnp.float32)
+    fourth = lax.rsqrt(lax.rsqrt(jnp.maximum(jnp.abs(code), SMALLEST)))
+    root = fourth * lax.rsqrt(fourth)
+    root = jnp.where(code > 0, root, jnp.where(code < 0, -root, 0.0))
+    return root * unit
+
+
+def kernel(cfg, x_hbm, out_ref, x_ref, own_t, got, part, code_out, code_in, *rest):
     depth, full, block, width, chunks, bits, n_aux, n_basis = cfg
-    hop_refs = rest[: 2 * bits]
-    load_sem, ring_send, ring_recv, hop_send, hop_recv = rest[2 * bits :]
+    later = bits - 1
+    hop_refs = rest[: 2 * later]
+    load_sem, ring_send, ring_recv, hop_send, hop_recv = rest[2 * later :]
     half = width // 2
     rows = block // n_aux
     me_aux = lax.axis_index("aux")
@@ -67,9 +86,14 @@
 
     def hop_copy(n, side, hop):
         q = order(side)[hop]
+        if hop == 0:
+            source, target = code_out.at[n, side], code_in.at[n, side]
+        else:
+            source = part.at[(n, side) + cut(side, hop, True)]
+            target = hop_refs[side * later + hop - 1].at[n]
         return pltpu.make_async_remote_copy(
-            src_ref=part.at[(n, side) + cut(side, hop, True)],
-            dst_ref=hop_refs[side * bits + hop].at[n],
+            src_ref=source,
+            dst_ref=target,
             send_sem=hop_send.at[n, side, hop],
             recv_sem=hop_recv.at[n, side, hop],
             device_id={"aux": partner[q]},
@@ -87,6 +111,7 @@
 
     tiles = [(s, j) for s in range(SHIFTS) for j in range(chunks)]
     lhs_rows = min(256, block)
+    sent = block // 2
 
     def compute(n):
         s, j = tiles[n]
@@ -106,16 +131,32 @@
                     part[(n, side) + tuple(index)] = product[
                         r * rows : (r + 1) * rows, side * half : (side + 1) * half
                     ]
-            return carry
-
-        lax.fori_loop(0, block // lhs_rows, body, 0)
+            size = jnp.abs(product).reshape(lhs_rows // 8, 8, width)
+            return jnp.maximum(carry, jnp.max(size, axis=0))
+
+        start = jnp.zeros((8, width), jnp.float32)
+        most = jnp.max(lax.fori_loop(0, block // lhs_rows, body, start))
+        unit = jnp.maximum(most, 2.0**-90) * 2.0**-14
+        for side in range(2):
+            tail = (n, side, pl.ds(sent, UNIT_ROWS))
+            code_out[tail] = jnp.full((UNIT_ROWS, half), unit).astype(jnp.bfloat16)
+            used = code_out[tail].astype(jnp.float32)[0:1]
+            value = part[(n, side) + cut(side, 0, True)].reshape(sent, half)
+            code_out[n, side, 0:sent] = encode(value, used)
+            hop_copy(n, side, 0).start()
 
     def finish(n, hop):
         s, j = tiles[n]
         for side in range(2):
             hop_copy(n, side, hop).wait_recv()
             index = (n, side) + cut(side, hop, False)
-            total = part[index] + hop_refs[side * bits + hop][n]
+            if hop == 0:
+                unit = code_in[n, side, sent:].astype(jnp.float32)[0:1]
+                arrived = decode(code_in[n, side, 0:sent], unit)
+                arrived = arrived.reshape((2,) * (bits - 1) + (rows, half))
+            else:
+                arrived = hop_refs[side * later + hop - 1][n]
+            total = part[index] + arrived
             if hop < bits - 1:
                 part[index] = total
                 hop_copy(n, side, hop + 1).start()
@@ -123,21 +164,25 @@
                 out_ref[s, :, j * width + side * half : j * width + (side + 1) * half] = total
 
     count = len(tiles)
-    lag = 2
-    for n in range(count + lag * bits):
-        if n < count:
-            s, j = tiles[n]
-            if s > 0:
-                ring_copy(s - 1, j).wait_recv()
-                if s < SHIFTS - 1:
-                    ring_copy(s, j).start()
-            compute(n)
-            for side in range(2):
-                hop_copy(n, side, 0).start()
+    done = {}
+
+    def catch_up(last, lag):
         for hop in range(bits):
-            m = n - lag * (hop + 1)
-            if 0 <= m < count:
+            for m in range(done.get(hop, 0), max(last - lag * hop + 1, 0)):
                 finish(m, hop)
+                done[hop] = m + 1
+
+    for n in range(count):
+        s, j = tiles[n]
+        if s > 0:
+            catch_up(n - 1, 0)
+            ring_copy(s - 1, j).wait_recv()
+            if s < SHIFTS - 1:
+                ring_copy(s, j).start()
+        compute(n)
+        if s == 0:
+            catch_up(n - 1, 1)
+    catch_up(count - 1, 0)
 
     for s in range(SHIFTS - 1):
         for j in range(chunks):
@@ -161,7 +206,7 @@
     half = width // 2
     hop_bufs = []
     for side in range(2):
-        for hop in range(bits):
+        for hop in range(1, bits):
             shape = (count,) + (2,) * (bits - 1 - hop) + (rows, half)
             hop_bufs.append(pltpu.VMEM(shape, jnp.float32))
     cfg = (depth, full, block, width, chunks, bits, n_aux, n_basis)
@@ -175,6 +220,8 @@
             pltpu.VMEM((block, full), jnp.bfloat16),
             pltpu.VMEM((SHIFTS - 1, full, block), jnp.bfloat16),
             pltpu.VMEM((count, 2) + (2,) * bits + (rows, half), jnp.float32),
+            pltpu.VMEM((count, 2, block // 2 + UNIT_ROWS, half), jnp.bfloat16),
+            pltpu.VMEM((count, 2, block // 2 + UNIT_ROWS, half), jnp.bfloat16),
             *hop_bufs,
             pltpu.SemaphoreType.DMA((chunks,)),
             pltpu.SemaphoreType.DMA((SHIFTS - 1, chunks)),

time: 124 us -> 134 us (1.081)
  the two profiles are of different devices: /device:TPU:1 before, /device:TPU:28 now
where the time goes in v3:
time: 134 us
  Pallas kernels  123 us (92%)
  local copies, waits for them, and re-layouts  11.4 us (9%)
    pallas_call x1, Pallas kernels, on_device(): pl.pallas_call(functools.partial(kernel, cfg), out_shape=jax.ShapeDtypeSt...  123 us
    reshape x1, local copies, waits for them, and re-layouts, on_device(): flat = jnp.transpose(factors, (1, 0, 2)).reshape(depth, block)  7.4 us
    unnamed x1, local copies, waits for them, and re-layouts  3.97 us

profile of v3, /device:TPU:28, one launch (start us, length us, event | category | flops | bytes accessed | tf_op | source)
XLA Modules:
  0.0 134.2 jit_solution(14966931667360268456)
XLA Ops:
  0.0 7.4 %reshape.3.x_hbm = bf16[2000,1024]{1,0:T(8,128)(2,1)} reshape(bf16[500,4,1024]{2,1,0:T(4,128)(2,1)} %bitcast.1) | data formatting | bytes 8192000 | tf_op jit(solution)/shard_map/reshape | solution.py:200
  7.4 122.8 %shard_map.17 = f32[3,256,1024]{2,1,0:T(8,128)} custom-call(bf16[2000,1024]{1,0:T(8,128)(2,1)} %reshape.3.x_hbm), custom_call_target="tpu_custom_call" | custom-call | flops 12884901888 | bytes 7340032 | tf_op jit(solution)/shard_map/pallas_call | solution.py:213
  130.2 4.0 %copy.3 = f32[3,256,1024]{2,1,0:T(8,128)} copy(f32[3,256,1024]{2,1,0:T(8,128)} %shard_map.17) | data formatting | bytes 6291456

commit v4 on v3

v4 whole, which is shorter than its diff:
```python
import functools

import jax
import jax.numpy as jnp
from jax import lax
from jax.experimental import pallas as pl
from jax.experimental.pallas import tpu as pltpu
from jax.sharding import PartitionSpec as P

SHIFTS = 3
AHEAD = 3
SMALLEST = 2.0**-125
UNIT_ROWS = 16
MESH = pl.DeviceIdType.MESH


def round_up(value, step):
    return -(-value // step) * step


def encode(value, unit):
    scaled = value * (1.0 / unit)
    power = scaled * scaled
    power = power * power
    power = power * power
    return jnp.where(scaled < 0, -power, power).astype(jnp.bfloat16)


def decode(code, unit):
    code = code.astype(jnp.float32)
    fourth = lax.rsqrt(lax.rsqrt(jnp.maximum(jnp.abs(code), SMALLEST)))
    root = fourth * lax.rsqrt(fourth)
    root = jnp.where(code > 0, root, jnp.where(code < 0, -root, 0.0))
    return root * unit


def kernel(cfg, x_hbm, out_ref, x_ref, own_t, got, part, code_out, code_in, *rest):
    depth, full, block, width, chunks, bits, n_aux, n_basis = cfg
    later = bits - 1
    hop_refs = rest[:later]
    load_sem, ring_send, ring_recv, hop_send, hop_recv = rest[later:]
    rows = block // n_aux
    me_aux = lax.axis_index("aux")
    me_basis = lax.axis_index("basis")
    left = lax.rem(me_basis + n_basis - 1, n_basis)
    right = lax.rem(me_basis + 1, n_basis)
    my_bit = [lax.rem(me_aux // (2**q), 2) for q in range(bits)]
    partner = [me_aux + (1 - 2 * my_bit[q]) * 2**q for q in range(bits)]

    def load(j):
        here = (pl.ds(0, depth), pl.ds(j * width, width))
        return pltpu.make_async_copy(x_hbm.at[here], x_ref.at[here], load_sem.at[j])

    for j in range(chunks):
        load(j).start()

    barrier = pltpu.get_barrier_semaphore()
    for who in [{"basis": left}, {"basis": right}] + [{"aux": p} for p in partner]:
        pl.semaphore_signal(barrier, inc=1, device_id=who, device_id_type=MESH)
    if full > depth:
        for s in range(SHIFTS - 1):
            got[s, depth:full, :] = jnp.zeros((full - depth, block), got.dtype)
        x_ref[depth:full, :] = jnp.zeros((full - depth, block), x_ref.dtype)
    pl.semaphore_wait(barrier, 2 + bits)

    def ring_copy(s, j):
        cols = pl.ds(j * width, width)
        source = x_ref if s == 0 else got.at[s - 1]
        return pltpu.make_async_remote_copy(
            src_ref=source.at[pl.ds(0, depth), cols],
            dst_ref=got.at[s, pl.ds(0, depth), cols],
            send_sem=ring_send.at[s, j],
            recv_sem=ring_recv.at[s, j],
            device_id={"basis": left},
            device_id_type=MESH,
        )

    def order(side):
        return list(range(bits)) if side == 0 else list(range(bits))[::-1]

    def cut(side, hop, last):
        index = [pl.ds(0, 2)] * bits
        for step, q in enumerate(order(side)[: hop + 1]):
            index[bits - 1 - q] = my_bit[q] if step < hop or not last else 1 - my_bit[q]
        return tuple(index)

    def hop_copy(n, hop):
        side = n % 2
        q = order(side)[hop]
        if hop == 0:
            source, target = code_out.at[n], code_in.at[n]
        else:
            source = part.at[(n,) + cut(side, hop, True)]
            target = hop_refs[hop - 1].at[n]
        return pltpu.make_async_remote_copy(
            src_ref=source,
            dst_ref=target,
            send_sem=hop_send.at[n, hop],
            recv_sem=hop_recv.at[n, hop],
            device_id={"aux": partner[q]},
            device_id_type=MESH,
        )

    pieces = [(s, j) for s in range(SHIFTS - 1) for j in range(chunks)]
    for j in range(chunks):
        load(j).wait()
        if j < AHEAD:
            ring_copy(*pieces[j]).start()

    step_cols = 128
    for i in range(block // step_cols):
        cols = pl.ds(i * step_cols, step_cols)
        own_t[cols, :] = x_ref[:, cols].T

    first = chunks // 2
    tiles = [(0, j) for j in range(first)]
    for i, piece in enumerate(pieces):
        tiles.append((piece[0] + 1, piece[1]))
        if first + i < chunks:
            tiles.append((0, first + i))
    lhs_rows = min(256, block)
    sent = block // 2

    def compute(n):
        s, j = tiles[n]
        cols = pl.ds(j * width, width)

        def body(i, carry):
            here = pl.ds(pl.multiple_of(i * lhs_rows, lhs_rows), lhs_rows)
            other = x_ref[:, cols] if s == 0 else got[s - 1, :, cols]
            product = jnp.dot(
                own_t[here, :], other, preferred_element_type=jnp.float32
            )
            per = lhs_rows // rows
            for r in range(per):
                g = i * per + r
                index = [lax.rem(g // (2**q), 2) for q in range(bits)][::-1]
                part[(n,) + tuple(index)] = product[r * rows : (r + 1) * rows]
            size = jnp.abs(product).reshape(lhs_rows // 8, 8, width)
            return jnp.maximum(carry, jnp.max(size, axis=0))

        start = jnp.zeros((8, width), jnp.float32)
        most = jnp.max(lax.fori_loop(0, block // lhs_rows, body, start))
        unit = jnp.maximum(most, 2.0**-90) * 2.0**-14
        tail = (n, pl.ds(sent, UNIT_ROWS))
        code_out[tail] = jnp.full((UNIT_ROWS, width), unit).astype(jnp.bfloat16)
        used = code_out[tail].astype(jnp.float32)[0:1]
        value = part[(n,) + cut(n % 2, 0, True)].reshape(sent, width)
        code_out[n, 0:sent] = encode(value, used)
        hop_copy(n, 0).start()

    def finish(n, hop):
        s, j = tiles[n]
        hop_copy(n, hop).wait_recv()
        index = (n,) + cut(n % 2, hop, False)
        if hop == 0:
            unit = code_in[n, sent:].astype(jnp.float32)[0:1]
            arrived = decode(code_in[n, 0:sent], unit)
            arrived = arrived.reshape((2,) * (bits - 1) + (rows, width))
        else:
            arrived = hop_refs[hop - 1][n]
        total = part[index] + arrived
        if hop < bits - 1:
            part[index] = total
            hop_copy(n, hop + 1).start()
        else:
            out_ref[s, :, j * width : (j + 1) * width] = total

    count = len(tiles)
    for n in range(count + bits):
        if n < count:
            s, j = tiles[n]
            if s > 0:
                tick = pieces.index((s - 1, j))
                ring_copy(s - 1, j).wait()
                if tick + AHEAD < len(pieces):
                    ring_copy(*pieces[tick + AHEAD]).start()
            compute(n)
        for hop in range(bits):
            if 0 <= n - 1 - hop < count:
                finish(n - 1 - hop, hop)

    for n in range(count):
        for hop in range(bits):
            hop_copy(n, hop).wait_send()


def on_device(n_aux, n_basis, factors):
    depth = factors.shape[0] * factors.shape[1]
    block = factors.shape[2]
    full = round_up(depth, 256)
    flat = jnp.transpose(factors, (1, 0, 2)).reshape(depth, block)
    bits = n_aux.bit_length() - 1
    width = 128
    chunks = block // width
    count = SHIFTS * chunks
    rows = block // n_aux
    hop_bufs = []
    for hop in range(1, bits):
        shape = (count,) + (2,) * (bits - 1 - hop) + (rows, width)
        hop_bufs.append(pltpu.VMEM(shape, jnp.float32))
    cfg = (depth, full, block, width, chunks, bits, n_aux, n_basis)
    return pl.pallas_call(
        functools.partial(kernel, cfg),
        out_shape=jax.ShapeDtypeStruct((SHIFTS, rows, block), jnp.float32),
        in_specs=[pl.BlockSpec(memory_space=pl.ANY)],
        out_specs=pl.BlockSpec(memory_space=pltpu.VMEM),
        scratch_shapes=[
            pltpu.VMEM((full, block), jnp.bfloat16),
            pltpu.VMEM((block, full), jnp.bfloat16),
            pltpu.VMEM((SHIFTS - 1, full, block), jnp.bfloat16),
            pltpu.VMEM((count,) + (2,) * bits + (rows, width), jnp.float32),
            pltpu.VMEM((count, block // 2 + UNIT_ROWS, width), jnp.bfloat16),
            pltpu.VMEM((count, block // 2 + UNIT_ROWS, width), jnp.bfloat16),
            *hop_bufs,
            pltpu.SemaphoreType.DMA((chunks,)),
            pltpu.SemaphoreType.DMA((SHIFTS - 1, chunks)),
            pltpu.SemaphoreType.DMA((SHIFTS - 1, chunks)),
            pltpu.SemaphoreType.DMA((count, bits)),
            pltpu.SemaphoreType.DMA((count, bits)),
        ],
        compiler_params=pltpu.CompilerParams(
            collective_id=0, has_side_effects=True, vmem_limit_bytes=58 * 2**20
        ),
        cost_estimate=pl.CostEstimate(
            flops=2 * SHIFTS * full * block * block,
            bytes_accessed=2 * full * block + 4 * SHIFTS * rows * block,
            transcendentals=0,
        ),
    )(flat)


def solution(mesh):
    n_aux, n_basis = mesh.shape["aux"], mesh.shape["basis"]
    return jax.shard_map(
        functools.partial(on_device, n_aux, n_basis),
        mesh=mesh,
        in_specs=(P("aux", None, "basis"),),
        out_specs=P(None, ("basis", "aux"), None),
        check_vma=False,
    )
```

time: 134 us -> 129 us (0.963)
  the two profiles are of different devices: /device:TPU:28 before, /device:TPU:1 now
where the time goes in v4:
time: 129 us
  Pallas kernels  117 us (91%)
  local copies, waits for them, and re-layouts  11.4 us (9%)
    pallas_call x1, Pallas kernels, on_device(): pl.pallas_call(functools.partial(kernel, cfg), out_shape=jax.ShapeDtypeSt...  117 us
    reshape x1, local copies, waits for them, and re-layouts, on_device(): flat = jnp.transpose(factors, (1, 0, 2)).reshape(depth, block)  7.4 us
    unnamed x1, local copies, waits for them, and re-layouts  3.97 us

profile of v4, /device:TPU:1, one launch (start us, length us, event | category | flops | bytes accessed | tf_op | source)
XLA Modules:
  0.0 128.8 jit_solution(10009626323456936188)
XLA Ops:
  0.0 7.4 %reshape.3.x_hbm = bf16[2000,1024]{1,0:T(8,128)(2,1)} reshape(bf16[500,4,1024]{2,1,0:T(4,128)(2,1)} %bitcast.1) | data formatting | bytes 8192000 | tf_op jit(solution)/shard_map/reshape | solution.py:192
  7.4 117.4 %shard_map.17 = f32[3,256,1024]{2,1,0:T(8,128)} custom-call(bf16[2000,1024]{1,0:T(8,128)(2,1)} %reshape.3.x_hbm), custom_call_target="tpu_custom_call" | custom-call | flops 12884901888 | bytes 7340032 | tf_op jit(solution)/shard_map/pallas_call | solution.py:203
  124.9 4.0 %copy.3 = f32[3,256,1024]{2,1,0:T(8,128)} copy(f32[3,256,1024]{2,1,0:T(8,128)} %shard_map.17) | data formatting | bytes 6291456

commit v5 on v3

--- a/solution.py
+++ b/solution.py
@@ -33,8 +33,9 @@
     return root * unit
 
 
-def kernel(cfg, x_hbm, out_ref, x_ref, own_t, got, part, code_out, code_in, *rest):
-    depth, full, block, width, chunks, bits, n_aux, n_basis = cfg
+def kernel(cfg, x_hbm, out_ref, x_ref, own_t, rhs, got, part, code_out, code_in, *rest):
+    inner, group, full, block, width, chunks, bits, n_aux, n_basis = cfg
+    depth = inner * group
     later = bits - 1
     hop_refs = rest[: 2 * later]
     load_sem, ring_send, ring_recv, hop_send, hop_recv = rest[2 * later :]
@@ -48,7 +49,7 @@
     partner = [me_aux + (1 - 2 * my_bit[q]) * 2**q for q in range(bits)]
 
     def load(j):
-        here = (pl.ds(0, depth), pl.ds(j * width, width))
+        here = (slice(None), slice(None), pl.ds(j * width, width))
         return pltpu.make_async_copy(x_hbm.at[here], x_ref.at[here], load_sem.at[j])
 
     for j in range(chunks):
@@ -58,17 +59,15 @@
     for who in [{"basis": left}, {"basis": right}] + [{"aux": p} for p in partner]:
         pl.semaphore_signal(barrier, inc=1, device_id=who, device_id_type=MESH)
     if full > depth:
-        for s in range(SHIFTS - 1):
-            got[s, depth:full, :] = jnp.zeros((full - depth, block), got.dtype)
-        x_ref[depth:full, :] = jnp.zeros((full - depth, block), x_ref.dtype)
+        rhs[depth:full, :] = jnp.zeros((full - depth, width), rhs.dtype)
     pl.semaphore_wait(barrier, 2 + bits)
 
     def ring_copy(s, j):
         cols = pl.ds(j * width, width)
         source = x_ref if s == 0 else got.at[s - 1]
         return pltpu.make_async_remote_copy(
-            src_ref=source.at[pl.ds(0, depth), cols],
-            dst_ref=got.at[s, pl.ds(0, depth), cols],
+            src_ref=source.at[:, :, cols],
+            dst_ref=got.at[s, :, :, cols],
             send_sem=ring_send.at[s, j],
             recv_sem=ring_recv.at[s, j],
             device_id={"basis": left},
@@ -104,10 +103,14 @@
         load(j).wait()
         ring_copy(0, j).start()
 
-    step_cols = 128
-    for i in range(block // step_cols):
-        cols = pl.ds(i * step_cols, step_cols)
-        own_t[cols, :] = x_ref[:, cols].T
+    def flatten(s, j):
+        source = x_ref if s == 0 else got.at[s - 1]
+        chunk = source[:, :, j * width : (j + 1) * width]
+        rhs[0:depth, :] = chunk.reshape(depth, width)
+
+    for j in range(chunks):
+        flatten(0, j)
+        own_t[j * width : (j + 1) * width, :] = rhs[...].T
 
     tiles = [(s, j) for s in range(SHIFTS) for j in range(chunks)]
     lhs_rows = min(256, block)
@@ -115,13 +118,12 @@
 
     def compute(n):
         s, j = tiles[n]
-        cols = pl.ds(j * width, width)
+        flatten(s, j)
 
         def body(i, carry):
             here = pl.ds(pl.multiple_of(i * lhs_rows, lhs_rows), lhs_rows)
-            other = x_ref[:, cols] if s == 0 else got[s - 1, :, cols]
             product = jnp.dot(
-                own_t[here, :], other, preferred_element_type=jnp.float32
+                own_t[here, :], rhs[...], preferred_element_type=jnp.float32
             )
             per = lhs_rows // rows
             for r in range(per):
@@ -175,13 +177,13 @@
     for n in range(count):
         s, j = tiles[n]
         if s > 0:
-            catch_up(n - 1, 0)
+            if s == SHIFTS - 1:
+                catch_up(n - 1, 0)
             ring_copy(s - 1, j).wait_recv()
             if s < SHIFTS - 1:
                 ring_copy(s, j).start()
         compute(n)
-        if s == 0:
-            catch_up(n - 1, 1)
+        catch_up(n - 1, 1)
     catch_up(count - 1, 0)
 
     for s in range(SHIFTS - 1):
@@ -194,10 +196,11 @@
 
 
 def on_device(n_aux, n_basis, factors):
-    depth = factors.shape[0] * factors.shape[1]
+    group, inner = factors.shape[0], factors.shape[1]
+    depth = inner * group
     block = factors.shape[2]
     full = round_up(depth, 256)
-    flat = jnp.transpose(factors, (1, 0, 2)).reshape(depth, block)
+    flat = jnp.transpose(factors, (1, 0, 2))
     bits = n_aux.bit_length() - 1
     width = 256
     chunks = block // width
@@ -209,16 +212,17 @@
         for hop in range(1, bits):
             shape = (count,) + (2,) * (bits - 1 - hop) + (rows, half)
             hop_bufs.append(pltpu.VMEM(shape, jnp.float32))
-    cfg = (depth, full, block, width, chunks, bits, n_aux, n_basis)
+    cfg = (inner, group, full, block, width, chunks, bits, n_aux, n_basis)
     return pl.pallas_call(
         functools.partial(kernel, cfg),
         out_shape=jax.ShapeDtypeStruct((SHIFTS, rows, block), jnp.float32),
         in_specs=[pl.BlockSpec(memory_space=pl.ANY)],
         out_specs=pl.BlockSpec(memory_space=pltpu.VMEM),
         scratch_shapes=[
-            pltpu.VMEM((full, block), jnp.bfloat16),
+            pltpu.VMEM((inner, group, block), jnp.bfloat16),
             pltpu.VMEM((block, full), jnp.bfloat16),
-            pltpu.VMEM((SHIFTS - 1, full, block), jnp.bfloat16),
+            pltpu.VMEM((full, width), jnp.bfloat16),
+            pltpu.VMEM((SHIFTS - 1, inner, group, block), jnp.bfloat16),
             pltpu.VMEM((count, 2) + (2,) * bits + (rows, half), jnp.float32),
             pltpu.VMEM((count, 2, block // 2 + UNIT_ROWS, half), jnp.bfloat16),
             pltpu.VMEM((count, 2, block // 2 + UNIT_ROWS, half), jnp.bfloat16),

time: 134 us -> 109 us (0.81)
  the two profiles are of different devices: /device:TPU:28 before, /device:TPU:1 now
where the time goes in v5:
time: 109 us
  Pallas kernels  105 us (96%)
  local copies, waits for them, and re-layouts  3.97 us (4%)
    pallas_call x1, Pallas kernels, on_device(): pl.pallas_call(functools.partial(kernel, cfg), out_shape=jax.ShapeDtypeSt...  105 us
    unnamed x1, local copies, waits for them, and re-layouts  3.97 us

profile of v5, /device:TPU:1, one launch (start us, length us, event | category | flops | bytes accessed | tf_op | source)
XLA Modules:
  0.0 109.3 jit_solution(5971734870947533289)
XLA Ops:
  0.0 105.3 %shard_map.17 = f32[3,256,1024]{2,1,0:T(8,128)} custom-call(bf16[500,4,1024]{2,1,0:T(4,128)(2,1)} %bitcast.1), custom_call_target="tpu_custom_call" | custom-call | flops 12884901888 | bytes 7340032 | tf_op jit(solution)/shard_map/pallas_call | solution.py:216
  105.3 4.0 %copy.3 = f32[3,256,1024]{2,1,0:T(8,128)} copy(f32[3,256,1024]{2,1,0:T(8,128)} %shard_map.17) | data formatting | bytes 6291456

commit v6 on v5

--- a/solution.py
+++ b/solution.py
@@ -33,12 +33,12 @@
     return root * unit
 
 
-def kernel(cfg, x_hbm, out_ref, x_ref, own_t, rhs, got, part, code_out, code_in, *rest):
+def kernel(cfg, x_hbm, out_hbm, x_ref, out_ref, own_t, rhs, got, part, code_out, code_in, *rest):
     inner, group, full, block, width, chunks, bits, n_aux, n_basis = cfg
     depth = inner * group
     later = bits - 1
     hop_refs = rest[: 2 * later]
-    load_sem, ring_send, ring_recv, hop_send, hop_recv = rest[2 * later :]
+    load_sem, store_sem, ring_send, ring_recv, hop_send, hop_recv = rest[2 * later :]
     half = width // 2
     rows = block // n_aux
     me_aux = lax.axis_index("aux")
@@ -62,14 +62,14 @@
         rhs[depth:full, :] = jnp.zeros((full - depth, width), rhs.dtype)
     pl.semaphore_wait(barrier, 2 + bits)
 
-    def ring_copy(s, j):
+    def ring_copy(s, j, low=0, high=inner):
         cols = pl.ds(j * width, width)
         source = x_ref if s == 0 else got.at[s - 1]
         return pltpu.make_async_remote_copy(
-            src_ref=source.at[:, :, cols],
-            dst_ref=got.at[s, :, :, cols],
-            send_sem=ring_send.at[s, j],
-            recv_sem=ring_recv.at[s, j],
+            src_ref=source.at[pl.ds(low, high - low), :, cols],
+            dst_ref=got.at[s, pl.ds(low, high - low), :, cols],
+            send_sem=ring_send.at[s, j if low == 0 else chunks],
+            recv_sem=ring_recv.at[s, j if low == 0 else chunks],
             device_id={"basis": left},
             device_id_type=MESH,
         )
@@ -103,10 +103,11 @@
         load(j).wait()
         ring_copy(0, j).start()
 
-    def flatten(s, j):
+    def flatten(s, j, low=0, high=inner):
         source = x_ref if s == 0 else got.at[s - 1]
-        chunk = source[:, :, j * width : (j + 1) * width]
-        rhs[0:depth, :] = chunk.reshape(depth, width)
+        chunk = source[low:high, :, j * width : (j + 1) * width]
+        chunk = chunk.reshape((high - low) * group, width)
+        rhs[low * group : high * group, :] = chunk
 
     for j in range(chunks):
         flatten(0, j)
@@ -115,29 +116,37 @@
     tiles = [(s, j) for s in range(SHIFTS) for j in range(chunks)]
     lhs_rows = min(256, block)
     sent = block // 2
-
-    def compute(n):
-        s, j = tiles[n]
-        flatten(s, j)
-
-        def body(i, carry):
+    middle = round_up(depth * 3 // 4, 256) // group
+
+    def multiply(n, low, high, add):
+        def body(i, most):
             here = pl.ds(pl.multiple_of(i * lhs_rows, lhs_rows), lhs_rows)
             product = jnp.dot(
-                own_t[here, :], rhs[...], preferred_element_type=jnp.float32
+                own_t[here, low:high],
+                rhs[low:high, :],
+                preferred_element_type=jnp.float32,
             )
             per = lhs_rows // rows
             for r in range(per):
                 g = i * per + r
                 index = [lax.rem(g // (2**q), 2) for q in range(bits)][::-1]
                 for side in range(2):
-                    part[(n, side) + tuple(index)] = product[
+                    place = (n, side) + tuple(index)
+                    value = product[
                         r * rows : (r + 1) * rows, side * half : (side + 1) * half
                     ]
-            size = jnp.abs(product).reshape(lhs_rows // 8, 8, width)
-            return jnp.maximum(carry, jnp.max(size, axis=0))
-
-        start = jnp.zeros((8, width), jnp.float32)
-        most = jnp.max(lax.fori_loop(0, block // lhs_rows, body, start))
+                    if add:
+                        value = value + part[place]
+                    part[place] = value
+                    size = jnp.abs(value).reshape(rows // 8, 8, half)
+                    most = jnp.maximum(most, jnp.max(size, axis=0))
+            return most
+
+        start = jnp.zeros((8, half), jnp.float32)
+        return lax.fori_loop(0, block // lhs_rows, body, start)
+
+    def send_first(n, most):
+        most = jnp.max(most)
         unit = jnp.maximum(most, 2.0**-90) * 2.0**-14
         for side in range(2):
             tail = (n, side, pl.ds(sent, UNIT_ROWS))
@@ -146,6 +155,11 @@
             value = part[(n, side) + cut(side, 0, True)].reshape(sent, half)
             code_out[n, side, 0:sent] = encode(value, used)
             hop_copy(n, side, 0).start()
+
+    def store(n):
+        s, j = tiles[n]
+        here = (s, slice(None), pl.ds(j * width, width))
+        return pltpu.make_async_copy(out_ref.at[here], out_hbm.at[here], store_sem.at[n])
 
     def finish(n, hop):
         s, j = tiles[n]
@@ -164,6 +178,8 @@
                 hop_copy(n, side, hop + 1).start()
             else:
                 out_ref[s, :, j * width + side * half : j * width + (side + 1) * half] = total
+        if hop == bits - 1:
+            store(n).start()
 
     count = len(tiles)
     done = {}
@@ -176,19 +192,37 @@
 
     for n in range(count):
         s, j = tiles[n]
+        split = n == count - 1
         if s > 0:
             if s == SHIFTS - 1:
                 catch_up(n - 1, 0)
-            ring_copy(s - 1, j).wait_recv()
-            if s < SHIFTS - 1:
+            ring_copy(s - 1, j, 0, middle if split else inner).wait_recv()
+            if s == SHIFTS - 2 and j == chunks - 1:
+                ring_copy(s, j, 0, middle).start()
+                ring_copy(s, j, middle, inner).start()
+            elif s < SHIFTS - 1:
                 ring_copy(s, j).start()
-        compute(n)
+        if split:
+            flatten(s, j, 0, middle)
+            multiply(n, 0, middle * group, False)
+            ring_copy(s - 1, j, middle, inner).wait_recv()
+            flatten(s, j, middle, inner)
+            send_first(n, multiply(n, middle * group, full, True))
+        else:
+            flatten(s, j)
+            send_first(n, multiply(n, 0, full, False))
         catch_up(n - 1, 1)
     catch_up(count - 1, 0)
 
     for s in range(SHIFTS - 1):
         for j in range(chunks):
-            ring_copy(s, j).wait_send()
+            if (s, j) == (SHIFTS - 2, chunks - 1):
+                ring_copy(s, j, 0, middle).wait_send()
+                ring_copy(s, j, middle, inner).wait_send()
+            else:
+                ring_copy(s, j).wait_send()
+    for n in range(count):
+        store(n).wait()
     for n in range(count):
         for side in range(2):
             for hop in range(bits):
@@ -217,9 +251,10 @@
         functools.partial(kernel, cfg),
         out_shape=jax.ShapeDtypeStruct((SHIFTS, rows, block), jnp.float32),
         in_specs=[pl.BlockSpec(memory_space=pl.ANY)],
-        out_specs=pl.BlockSpec(memory_space=pltpu.VMEM),
+        out_specs=pl.BlockSpec(memory_space=pl.ANY),
         scratch_shapes=[
             pltpu.VMEM((inner, group, block), jnp.bfloat16),
+            pltpu.VMEM((SHIFTS, rows, block), jnp.float32),
             pltpu.VMEM((block, full), jnp.bfloat16),
             pltpu.VMEM((full, width), jnp.bfloat16),
             pltpu.VMEM((SHIFTS - 1, inner, group, block), jnp.bfloat16),
@@ -228,8 +263,9 @@
             pltpu.VMEM((count, 2, block // 2 + UNIT_ROWS, half), jnp.bfloat16),
             *hop_bufs,
             pltpu.SemaphoreType.DMA((chunks,)),
-            pltpu.SemaphoreType.DMA((SHIFTS - 1, chunks)),
-            pltpu.SemaphoreType.DMA((SHIFTS - 1, chunks)),
+            pltpu.SemaphoreType.DMA((count,)),
+            pltpu.SemaphoreType.DMA((SHIFTS - 1, chunks + 1)),
+            pltpu.SemaphoreType.DMA((SHIFTS - 1, chunks + 1)),
             pltpu.SemaphoreType.DMA((count, 2, bits)),
             pltpu.SemaphoreType.DMA((count, 2, bits)),
         ],

time: 109 us -> 108 us (level)
    pallas_call x1, Pallas kernels: 105 us -> 104 us  [on_device(): pl.pallas_call(functools.partial(kernel, cfg), out_shape=jax.ShapeDtypeSt...]
where the time goes in v6:
time: 108 us
  Pallas kernels  104 us (96%)
  local copies, waits for them, and re-layouts  3.97 us (4%)
    pallas_call x1, Pallas kernels, on_device(): pl.pallas_call(functools.partial(kernel, cfg), out_shape=jax.ShapeDtypeSt...  104 us
    unnamed x1, local copies, waits for them, and re-layouts  3.97 us

profile of v6, /device:TPU:1, one launch (start us, length us, event | category | flops | bytes accessed | tf_op | source)
XLA Modules:
  0.0 108.1 jit_solution(14935969396171674615)
XLA Ops:
  0.0 104.2 %shard_map.17 = f32[3,256,1024]{2,1,0:T(8,128)} custom-call(bf16[500,4,1024]{2,1,0:T(4,128)(2,1)} %bitcast.1), custom_call_target="tpu_custom_call" | custom-call | flops 12884901888 | bytes 7340032 | tf_op jit(solution)/shard_map/pallas_call | solution.py:250
  104.2 4.0 %copy.3 = f32[3,256,1024]{2,1,0:T(8,128)} copy(f32[3,256,1024]{2,1,0:T(8,128)} %shard_map.17) | data formatting | bytes 6291456

commit v7 on v6

--- a/solution.py
+++ b/solution.py
@@ -229,6 +229,20 @@
                 hop_copy(n, side, hop).wait_send()
 
 
+def hand_on(parts, source, target, sems):
+    per = source.shape[1] // parts
+    copies = []
+    for s in range(SHIFTS):
+        for i in range(parts):
+            here = (s, pl.ds(i * per, per))
+            sem = sems.at[s * parts + i]
+            copies.append(pltpu.make_async_copy(source.at[here], target.at[here], sem))
+    for copy in copies:
+        copy.start()
+    for copy in copies:
+        copy.wait()
+
+
 def on_device(n_aux, n_basis, factors):
     group, inner = factors.shape[0], factors.shape[1]
     depth = inner * group
@@ -247,7 +261,7 @@
             shape = (count,) + (2,) * (bits - 1 - hop) + (rows, half)
             hop_bufs.append(pltpu.VMEM(shape, jnp.float32))
     cfg = (inner, group, full, block, width, chunks, bits, n_aux, n_basis)
-    return pl.pallas_call(
+    result = pl.pallas_call(
         functools.partial(kernel, cfg),
         out_shape=jax.ShapeDtypeStruct((SHIFTS, rows, block), jnp.float32),
         in_specs=[pl.BlockSpec(memory_space=pl.ANY)],
@@ -278,6 +292,17 @@
             transcendentals=0,
         ),
     )(flat)
+    parts = 4 if rows % 32 == 0 else 1
+    return pl.pallas_call(
+        functools.partial(hand_on, parts),
+        out_shape=jax.ShapeDtypeStruct(result.shape, result.dtype),
+        in_specs=[pl.BlockSpec(memory_space=pl.ANY)],
+        out_specs=pl.BlockSpec(memory_space=pl.ANY),
+        scratch_shapes=[pltpu.SemaphoreType.DMA((SHIFTS * parts,))],
+        cost_estimate=pl.CostEstimate(
+            flops=0, bytes_accessed=8 * SHIFTS * rows * block, transcendentals=0
+        ),
+    )(result)
 
 
 def solution(mesh):

time: 108 us -> 201 us (1.86)
  Pallas kernels: 104 us -> 201 us
  local copies, waits for them, and re-layouts: 3.97 us -> 0 us
    pallas_call x0 -> x1, Pallas kernels: none -> 96.5 us  [on_device(): pl.pallas_call(functools.partial(hand_on, parts), out_shape=jax.ShapeDtyp...]
    unnamed x1 -> x0, local copies, waits for them, and re-layouts: 3.97 us -> none
where the time goes in v7:
time: 201 us
  Pallas kernels  201 us (100%)
    pallas_call x1, Pallas kernels, on_device(): pl.pallas_call(functools.partial(kernel, cfg), out_shape=jax.ShapeDtypeSt...  104 us
    pallas_call x1, Pallas kernels, on_device(): pl.pallas_call(functools.partial(hand_on, parts), out_shape=jax.ShapeDtyp...  96.5 us

profile of v7, /device:TPU:1, one launch (start us, length us, event | category | flops | bytes accessed | tf_op | source)
XLA Modules:
  0.0 200.7 jit_solution(13147585730459959369)
XLA Ops:
  0.0 104.2 %shard_map.17.source = f32[3,256,1024]{2,1,0:T(8,128)} custom-call(bf16[500,4,1024]{2,1,0:T(4,128)(2,1)} %bitcast.1), custom_call_target="tpu_custom_call" | custom-call | flops 12884901888 | bytes 7340032 | tf_op jit(solution)/shard_map/pallas_call | solution.py:264
  104.2 96.5 %shard_map.18 = f32[3,256,1024]{2,1,0:T(8,128)} custom-call(f32[3,256,1024]{2,1,0:T(8,128)} %shard_map.17.source), custom_call_target="tpu_custom_call" | custom-call | bytes 6291456 | tf_op jit(solution)/shard_map/pallas_call | solution.py:296

commit v8 on v7

--- a/solution.py
+++ b/solution.py
@@ -229,18 +229,22 @@
                 hop_copy(n, side, hop).wait_send()
 
 
-def hand_on(parts, source, target, sems):
+def hand_on(parts, source, target, held, sems):
     per = source.shape[1] // parts
-    copies = []
+    pairs = []
     for s in range(SHIFTS):
         for i in range(parts):
-            here = (s, pl.ds(i * per, per))
-            sem = sems.at[s * parts + i]
-            copies.append(pltpu.make_async_copy(source.at[here], target.at[here], sem))
-    for copy in copies:
-        copy.start()
-    for copy in copies:
-        copy.wait()
+            here, k = (s, pl.ds(i * per, per)), s * parts + i
+            into = pltpu.make_async_copy(source.at[here], held.at[here], sems.at[0, k])
+            out = pltpu.make_async_copy(held.at[here], target.at[here], sems.at[1, k])
+            pairs.append((into, out))
+    for into, _ in pairs:
+        into.start()
+    for into, out in pairs:
+        into.wait()
+        out.start()
+    for _, out in pairs:
+        out.wait()
 
 
 def on_device(n_aux, n_basis, factors):
@@ -298,7 +302,11 @@
         out_shape=jax.ShapeDtypeStruct(result.shape, result.dtype),
         in_specs=[pl.BlockSpec(memory_space=pl.ANY)],
         out_specs=pl.BlockSpec(memory_space=pl.ANY),
-        scratch_shapes=[pltpu.SemaphoreType.DMA((SHIFTS * parts,))],
+        scratch_shapes=[
+            pltpu.VMEM(result.shape, result.dtype),
+            pltpu.SemaphoreType.DMA((2, SHIFTS * parts)),
+        ],
+        compiler_params=pltpu.CompilerParams(vmem_limit_bytes=58 * 2**20),
         cost_estimate=pl.CostEstimate(
             flops=0, bytes_accessed=8 * SHIFTS * rows * block, transcendentals=0
         ),

time: 201 us -> 107 us (0.53)
  Pallas kernels: 201 us -> 107 us
    pallas_call x1, Pallas kernels: 96.5 us -> 2.81 us  [on_device(): pl.pallas_call(functools.partial(hand_on, parts), out_shape=jax.ShapeDtyp...]
where the time goes in v8:
time: 107 us
  Pallas kernels  107 us (100%)
    pallas_call x1, Pallas kernels, on_device(): pl.pallas_call(functools.partial(kernel, cfg), out_shape=jax.ShapeDtypeSt...  104 us
    pallas_call x1, Pallas kernels, on_device(): pl.pallas_call(functools.partial(hand_on, parts), out_shape=jax.ShapeDtyp...  2.81 us

profile of v8, /device:TPU:1, one launch (start us, length us, event | category | flops | bytes accessed | tf_op | source)
XLA Modules:
  0.0 107.0 jit_solution(6056839568791421408)
XLA Ops:
  0.0 104.2 %shard_map.17.source = f32[3,256,1024]{2,1,0:T(8,128)} custom-call(bf16[500,4,1024]{2,1,0:T(4,128)(2,1)} %bitcast.1), custom_call_target="tpu_custom_call" | custom-call | flops 12884901888 | bytes 7340032 | tf_op jit(solution)/shard_map/pallas_call | solution.py:268
  104.2 2.8 %shard_map.18 = f32[3,256,1024]{2,1,0:T(8,128)} custom-call(f32[3,256,1024]{2,1,0:T(8,128)} %shard_map.17.source), custom_call_target="tpu_custom_call" | custom-call | bytes 6291456 | tf_op jit(solution)/shard_map/pallas_call | solution.py:300

commit v9 on v8

--- a/solution.py
+++ b/solution.py
@@ -116,7 +116,7 @@
     tiles = [(s, j) for s in range(SHIFTS) for j in range(chunks)]
     lhs_rows = min(256, block)
     sent = block // 2
-    middle = round_up(depth * 3 // 4, 256) // group
+    middle = round_up(depth * 7 // 8 - 128, 256) // group
 
     def multiply(n, low, high, add):
         def body(i, most):

time: 107 us -> 107 us (level)
  no operation moved by 1% of the time
where the time goes in v9:
time: 107 us
  Pallas kernels  107 us (100%)
    pallas_call x1, Pallas kernels, on_device(): pl.pallas_call(functools.partial(kernel, cfg), out_shape=jax.ShapeDtypeSt...  104 us
    pallas_call x1, Pallas kernels, on_device(): pl.pallas_call(functools.partial(hand_on, parts), out_shape=jax.ShapeDtyp...  2.81 us

profile of v9, /device:TPU:1, one launch (start us, length us, event | category | flops | bytes accessed | tf_op | source)
XLA Modules:
  0.0 107.1 jit_solution(13496925316305499901)
XLA Ops:
  0.0 104.3 %shard_map.17.source = f32[3,256,1024]{2,1,0:T(8,128)} custom-call(bf16[500,4,1024]{2,1,0:T(4,128)(2,1)} %bitcast.1), custom_call_target="tpu_custom_call" | custom-call | flops 12884901888 | bytes 7340032 | tf_op jit(solution)/shard_map/pallas_call | solution.py:268
  104.3 2.8 %shard_map.18 = f32[3,256,1024]{2,1,0:T(8,128)} custom-call(f32[3,256,1024]{2,1,0:T(8,128)} %shard_map.17.source), custom_call_target="tpu_custom_call" | custom-call | bytes 6291456 | tf_op jit(solution)/shard_map/pallas_call | solution.py:300
